TPU v7x, 512 devices: a whole 4x8x8 slice. The times are simulated.
512 devices in a mesh: lat: 16 (over z, x_hi), lon: 32 (over x_lo, y, core).
Axes of the slice: x: 4 (x_hi: 2, x_lo: 2; x = x_hi * 2 + x_lo), y: 8, z: 8, core: 2. Of those that a mesh axis runs over, the one named last changes fastest.
Arguments:
- fine_tokens: bfloat16 [2, 192, 384, 192], P(None, 'lat', 'lon'), may hold values from -6 to 6
- ln1_gain: float32 [192], replicated, may hold values from 0.1 to 1.9
- w_qkv1: bfloat16 [192, 576], replicated, may hold values from -6.928203 to 6.928203
- bias1: float32 [32, 1, 6, 3312], P('lat'), may hold values from -4 to 4
- w_proj1: bfloat16 [192, 192], replicated, may hold values from -0.4375 to 0.4375
- ln2_gain: float32 [192], replicated, may hold values from 0.1 to 1.9
- w_fc1: bfloat16 [192, 768], replicated, may hold values from -0.4375 to 0.4375
- w_fc2: bfloat16 [768, 192], replicated, may hold values from -0.21875 to 0.21875
- merge_gain: float32 [768], replicated, may hold values from 0.1 to 1.9
- w_merge: bfloat16 [768, 384], replicated, may hold values from -0.21875 to 0.21875
- ln3_gain: float32 [384], replicated, may hold values from 0.1 to 1.9
- w_qkv2: bfloat16 [384, 1152], replicated, may hold values from -4.8989795 to 4.8989795
- bias2: float32 [16, 1, 12, 3312], P('lat'), may hold values from -4 to 4
- w_proj2: bfloat16 [384, 384], replicated, may hold values from -0.3125 to 0.3125
Outputs:
- fine_out: bfloat16 [2, 192, 384, 192], P(None, 'lat', 'lon')
- coarse_out: bfloat16 [2, 96, 192, 384], P(None, 'lat', 'lon')
All inputs are finite; a program needn't handle non-finite values.
Results may differ from a plain program's by a relative error of at most 0.039.
Values may be sent and summed in bfloat16 or wider, within the bound.
A program may use at most 128 MiB of HBM per device.

v0:
```python
import functools
from types import SimpleNamespace

import jax
import jax.numpy as jnp
import numpy as np
from jax import lax
from jax.experimental import pallas as pl
from jax.experimental.pallas import tpu as pltpu
from jax.sharding import PartitionSpec as P

MESH = pl.DeviceIdType.MESH
F32 = jnp.float32
BF16 = jnp.bfloat16
SCALE = 32 ** (-0.5)

SEG = dict(LC=0, LB=64, LA=176, RA=240, RB=304, RC=416, LC2=480)
SEG_ROWS = 544
TALL = dict(A=64, B=112, C=64)
SIDE = dict(A=40, B=72, C=40)
HALO = {
    "W.RA": 0, "W.RB": 64, "W.RC": 176,
    "E.LC": 240, "E.LB": 304, "E.LA": 416,
    "N.RC": 480, "N.LC": 544,
    "S.LA": 608, "S.RA": 672,
    "NW.RC": 736, "NE.LC": 800, "SW.RA": 864, "SE.LA": 928,
}
HALO_ROWS = 992
MESSAGES = (
    (0, -1, 0, 240, 240),
    (0, 1, 240, 240, 0),
    (-1, 0, 176, 128, 608),
    (1, 0, 416, 128, 480),
    (-1, -1, 176, 64, 928),
    (-1, 1, 240, 64, 864),
    (1, -1, 0, 64, 800),
    (1, 1, 416, 64, 736),
)
WINDOWS = dict(
    LB=("W.RB", "LB"),
    RB=("RB", "E.LB"),
    LC=("W.RC", "SW.RA", "LC", "S.LA"),
    RC=("RC", "S.RA", "E.LC", "SE.LA"),
    LA=("NW.RC", "W.RA", "N.LC", "LA"),
    RA=("N.RC", "RA", "NE.LC", "E.LA"),
)
SLOT = dict(LA=0, LB=256, LC=768, RA=1024, RB=1280, RC=1792)
LANES = 2048
FIRST_ROW = dict(A=0, B=3, C=9)
ROWS = dict(A=3, B=6, C=3)


def fine_row(level, row, col):
    return (row % 2 * 2 + col % 2) * 72 + col // 2 * 12 + row // 2 * 2 + level


@functools.cache
def tables():
    seg = np.zeros((SEG_ROWS, 288), np.float32)
    perm = np.zeros((288, 288), np.float32)
    for name, start in SEG.items():
        group = name[1]
        for turned in range(2):
            for col in range(6):
                for row in range(ROWS[group]):
                    place = start + (turned * 6 + col) * ROWS[group] + row
                    own_col = col + (0 if name[0] == "L" else 6)
                    source = ((FIRST_ROW[group] + row) * 12 + own_col) * 2 + 1 - turned
                    seg[place, source] = 1
                    seg[start + SIDE[group] + col * ROWS[group] + row, source] = 1
    for level in range(2):
        for row in range(12):
            for col in range(12):
                perm[fine_row(level, row, col), (row * 12 + col) * 2 + level] = 1
    spread = np.zeros((LANES, 288), np.float32)
    for name, start in SLOT.items():
        group = name[1]
        many = ROWS[group]
        for turned in range(2):
            for col in range(6):
                for head in range(6):
                    for row in range(many):
                        lane = start + turned * (128 if many == 3 else 256)
                        lane = lane + (col * 6 + head) * many + row
                        own_col = col + (0 if name[0] == "L" else 6)
                        spread[lane, fine_row(1 - turned, FIRST_ROW[group] + row, own_col)] = 1
    head_rows = np.zeros((384, 192), np.float32)
    for many, base in ((3, 0), (6, 128)):
        for lane in range(36 * many):
            head = lane // many % 6
            head_rows[base + lane, head * 32 : head * 32 + 32] = 1
    gather_a = np.zeros((216, 256), np.float32)
    gather_b = np.zeros((216, 224), np.float32)
    for level in range(2):
        for col in range(12):
            for row in range(6):
                key = level * 72 + col * 6 + row
                part = col // 6 * 2 + row // 3
                place = col % 6 * 3 + row % 3
                gather_a[key, part * 64 + level * 18 + place] = 1
                gather_a[144 + col * 6 + row, part * 64 + 40 + place] = 1
                place = col % 6 * 6 + row
                gather_b[key, col // 6 * 112 + level * 36 + place] = 1
                gather_b[144 + col * 6 + row, col // 6 * 112 + 72 + place] = 1
    pick = np.zeros((96, 256), np.float32)
    for rq in range(6):
        for level in range(2):
            for rk in range(6):
                pick[rq * 16 + level * 8 + rk, rq * 24 + rk * 4 + level * 3] = 1
    rep_b = np.zeros((184, 896), np.float32)
    rep_a = np.zeros((184, 512), np.float32)
    lane_b = np.zeros((8, 896), np.float32)
    lane_a = np.zeros((8, 512), np.float32)
    for step in range(23):
        for head in range(6):
            for row in range(6):
                lane = step * 36 + head * 6 + row
                rep_b[step * 8 + head, lane] = 1
                lane_b[row, lane] = 1
            for row in range(3):
                lane = step * 18 + head * 3 + row
                rep_a[step * 8 + head, lane] = 1
                lane_a[row, lane] = 1
    pick2 = np.zeros((192, 256), np.float32)
    for rq in range(6):
        for rk in range(6):
            for zq in range(2):
                for zk in range(2):
                    pick2[(rq * 2 + zq) * 16 + rk * 2 + zk, rq * 24 + rk * 4 + zq * 2 + zk] = 1
    rep_c = np.zeros((176, 1664), np.float32)
    lane_c = np.zeros((16, 1664), np.float32)
    for step in range(11):
        for head in range(12):
            for token in range(12):
                lane = step * 144 + head * 12 + token
                rep_c[step * 16 + head, lane] = 1
                lane_c[token, lane] = 1
    spread2 = np.zeros((896, 128), np.float32)
    head_rows2 = np.zeros((896, 384), np.float32)
    for col in range(6):
        for head in range(12):
            for token in range(12):
                lane = col * 144 + head * 12 + token
                spread2[lane, col * 12 + token] = 1
                head_rows2[lane, head * 32 : head * 32 + 32] = 1
    pad2 = np.zeros((80, 128), np.float32)
    for level in range(2):
        for row in range(6):
            for col in range(6):
                pad2[(row * 6 + col) * 2 + level, col * 12 + row * 2 + level] = 1
    return dict(
        seg=seg, perm=perm, spread=spread, head_rows=head_rows,
        pick=pick, rep_a=rep_a, lane_a=lane_a, rep_b=rep_b, lane_b=lane_b,
        pick2=pick2, rep_c=rep_c, lane_c=lane_c,
        gather_a=gather_a, gather_b=gather_b, head_cols=head_rows.T,
        collect=spread.T, unperm=perm.T, spread2=spread2, head_rows2=head_rows2,
        head_cols2=head_rows2.T, collect2=pad2 @ spread2.T, pad2=pad2,
    )


LAST = ("perm", "head_rows", "lane_b", "lane_c", "pad2")


@functools.cache
def packed():
    parts, place, row = [], {}, 0
    for name, value in tables().items():
        rows, lanes = value.shape
        tall = -(-rows // 16) * 16
        wide = -(-lanes // 128)
        padded = np.zeros((tall, wide * 128), np.float32)
        padded[:rows, :lanes] = value
        place[name] = (row, rows, tall, lanes, wide)
        for column in range(wide):
            parts.append(padded[:, column * 128 : column * 128 + 128])
        row += tall * wide
    ends = [0] + [place[name][0] + place[name][2] * place[name][4] for name in LAST]
    ranges = list(zip(ends, ends[1:]))
    return np.concatenate(parts).astype(jnp.bfloat16), place, ranges


LOADED = (
    "fine_tokens", "ln1_gain", 0, "w_qkv1", 1, 2, 3, 4, "w_proj1", "ln2_gain", "w_fc1", "w_fc2",
    "merge_gain", "w_merge", "ln3_gain", "w_qkv2", "w_proj2",
)
KEPT = tuple(name for name in LOADED if isinstance(name, str))


def mul(a, b):
    return lax.dot_general(a, b, (((1,), (0,)), ((), ())), preferred_element_type=F32)


def mul_t(a, b):
    return lax.dot_general(a, b, (((1,), (1,)), ((), ())), preferred_element_type=F32)


def norm(v, gain):
    average = jnp.mean(v, axis=-1, keepdims=True)
    centred = v - average
    spread = jnp.mean(centred * centred, axis=-1, keepdims=True)
    return centred * lax.rsqrt(spread + 1e-05) * gain


def shifted(v, start, width):
    base = start // 128 * 128
    window = -(-(start - base + width) // 128) * 128
    part = v[:, base : base + window]
    if start == base:
        return part[:, :width]
    return pltpu.roll(part, window - (start - base), 1)[:, :width]


def by_step(table, steps):
    return jnp.concatenate([by_one(table, step) for step in range(steps)], axis=0)


def by_one(table, d):
    start = d * 144
    base = start // 128 * 128
    part = table[:, base : base + 256]
    if start == base:
        return part
    return pltpu.roll(part, 256 - (start - base), 1)


def below(v, rows):
    return jnp.concatenate([v, jnp.zeros((rows - v.shape[0], v.shape[1]), F32)], axis=0).astype(BF16)


def split(v):
    high = v.astype(BF16)
    return high, (v - high.astype(F32)).astype(BF16)


def picked(pick, rows):
    return mul_t(pick, rows).astype(BF16)


def merged(parts, rep, lanes):
    wide = [mul(part, rep) for part in parts]
    total = None
    for token in range(parts[0].shape[0] // 16):
        term = sum(w[token * 16 : token * 16 + 16] for w in wide) * lanes[token : token + 1]
        total = term if total is None else total + term
    return total


def kernel(names, *refs):
    count = len(names)
    ops = SimpleNamespace(**dict(zip(names, refs[:count])))
    fine_ref, coarse_ref = refs[count : count + 2]
    rest = list(refs[count + 2 :])
    loaded = SimpleNamespace(**dict(zip(KEPT, rest[: len(KEPT)])))
    (pack, tab, tab2, own_rows, segs, halo, table_sent, table_got, table_in, table_2, queries, bias,
     bias2, mixed, rows_sent, rows_got, fine_buf, coarse_buf, load_sem, tab_sem, out_sem, send_sem,
     recv_sem) = rest[len(KEPT) :]
    _, place, ranges = packed()

    lat, lon = lax.axis_index("lat"), lax.axis_index("lon")
    lats, lons = lax.axis_size("lat"), lax.axis_size("lon")

    def at(dlat, dlon):
        return (lax.rem(lat + dlat + lats, lats), lax.rem(lon + dlon + lons, lons))

    copies = {}
    for number, name in enumerate(LOADED):
        if isinstance(name, str):
            source, target = getattr(ops, name), getattr(loaded, name)
        else:
            rows = pl.ds(ranges[name][0], ranges[name][1] - ranges[name][0])
            source, target = ops.pack.at[rows], pack.at[rows]
        copies[name] = pltpu.make_async_copy(source, target, load_sem.at[number])
    tables_in = [
        pltpu.make_async_copy(ops.bias1, table_in, tab_sem.at[0]),
        pltpu.make_async_copy(ops.bias2, table_2, tab_sem.at[1]),
    ]
    for name in LOADED[:3]:
        copies[name].start()

    barrier = pltpu.get_barrier_semaphore()
    for dlat, dlon, _, _, _ in MESSAGES:
        pl.semaphore_signal(barrier, inc=1, device_id=at(dlat, dlon), device_id_type=MESH)
    for copy in tables_in:
        copy.start()
    for name in LOADED[3:]:
        copies[name].start()

    def arrived(name):
        copies[name].wait()
        return getattr(loaded, name)

    get = SimpleNamespace(**{name: functools.partial(arrived, name) for name in KEPT})

    def table(name):
        first, rows, tall, lanes, wide = place[name]
        parts = [pack[first + tall * c : first + tall * c + rows, :] for c in range(wide)]
        value = parts[0] if wide == 1 else jnp.concatenate(parts, axis=1)
        return value[:, :lanes]

    const = SimpleNamespace(**{name: functools.partial(table, name) for name in place})

    gain1 = get.ln1_gain()[...]
    own_tokens = get.fine_tokens()
    for token in range(144):
        own_rows[token * 2 : token * 2 + 2, :] = own_tokens[token].astype(F32)
    raw = own_rows[...]
    normed = norm(raw, gain1)
    level = lax.broadcasted_iota(jnp.int32, (288, 1), 0) % 2
    side = jnp.concatenate([normed[:, 128:], jnp.zeros((288, 64), F32)], axis=1)
    side = jnp.where(level == 1, side, pltpu.roll(side, 64, 1))
    normed = normed.astype(BF16)
    copies[0].wait()
    cut = mul(const.seg(), jnp.concatenate([normed[:, :128], side.astype(BF16)], axis=1))
    pieces = []
    for name, first in SEG.items():
        middle, end = first + SIDE[name[1]], first + TALL[name[1]]
        pieces += [cut[first:middle, :128], cut[middle:end, 128:]]
    segs[...] = jnp.concatenate(pieces, axis=0).astype(BF16)

    pl.semaphore_wait(barrier, len(MESSAGES))
    sends = []
    for number, (dlat, dlon, first, many, there) in enumerate(MESSAGES):
        sends.append(
            pltpu.make_async_remote_copy(
                src_ref=segs.at[pl.ds(first, many)], dst_ref=halo.at[pl.ds(there, many)],
                send_sem=send_sem.at[number], recv_sem=recv_sem.at[number],
                device_id=at(dlat, dlon), device_id_type=MESH,
            )
        )
    for number in (2, 3, 4, 5, 6, 7, 0, 1):
        sends[number].start()

    tables_in[0].wait()
    copies[2].wait()
    tab[...] = jnp.zeros_like(tab)
    pick = const.pick()

    def steps_of(first_head):
        for head in range(6):
            tab[head : head + 1, :3312] = table_in[first_head + head]
        return split(by_step(tab[...], 23))

    high, low = steps_of(6)
    high = picked(pick, high)
    table_sent[...] = high[48:]
    table_copy = pltpu.make_async_remote_copy(
        src_ref=table_sent, dst_ref=table_got, send_sem=send_sem.at[8], recv_sem=recv_sem.at[8],
        device_id=at(1, 0), device_id_type=MESH,
    )
    table_copy.start()
    parts_c = (high[:48], picked(pick[:48], low))
    high, low = steps_of(0)
    parts_b = (picked(pick, high), picked(pick, low))
    rep_a, lane_a = const.rep_a(), const.lane_a().astype(F32)
    key_row = lax.broadcasted_iota(jnp.int32, (16, 1), 0) % 8

    def lay_bias(group, value):
        per_col = 6 * ROWS[group]
        wide = 128 if group != "B" else 256
        for half in "LR":
            start = SLOT[half + group]
            for key_col in range(12):
                first = ((17 if half == "L" else 11) - key_col) * per_col
                part = shifted(value, first, wide)
                for level in range(2):
                    lo = start + level * wide
                    bias[key_col * 6 : key_col * 6 + 6, lo : lo + wide] = part[level * 8 : level * 8 + 6]

    lay_bias("B", merged(parts_b, const.rep_b(), const.lane_b().astype(F32)))
    value = merged(parts_c, rep_a, lane_a)
    lay_bias("C", jnp.where(jnp.logical_and(key_row >= 3, lat == lats - 1), -1e9, value))

    own = mul(const.perm(), raw.astype(BF16))
    own_normed = mul(const.perm(), normed).astype(BF16)
    w_qkv1 = get.w_qkv1()[...]
    own_queries = mul(own_normed, w_qkv1[:, :192]).astype(BF16)
    w_key = pltpu.roll(w_qkv1[:, 128:384].astype(F32), 192, 1)[:, :192].astype(BF16)
    w_value = w_qkv1[:, 384:]

    def unit(size):
        rows = lax.broadcasted_iota(jnp.int32, (size, size), 0)
        cols = lax.broadcasted_iota(jnp.int32, (size, size), 1)
        return jnp.where(rows == cols, 1.0, 0.0).astype(BF16)

    def placed(w, level):
        zeros = jnp.zeros((64, w.shape[1]), BF16)
        tail = (w[128:], zeros) if level == 0 else (zeros, w[128:])
        return jnp.concatenate((w[:128],) + tail, axis=0)

    w_keys = [placed(w_key, level) for level in range(2)]
    w_values_t = [mul_t(unit(192), placed(w_value, level)).astype(BF16) for level in range(2)]
    copies[1].wait()
    spread = const.spread()
    head_rows = const.head_rows().astype(F32)
    for name, start in SLOT.items():
        wide = 128 if name[1] != "B" else 256
        mask = head_rows[:128] if name[1] != "B" else head_rows[128:]
        for level in range(2):
            lo = start + level * wide
            queries[lo : lo + wide, :] = (mul(spread[lo : lo + wide], own_queries) * mask).astype(BF16)

    copies[4].wait()
    gathers = dict(A=const.gather_a(), B=const.gather_b())
    gathers.update(C=gathers["A"])
    head_cols = const.head_cols().astype(F32)

    def attend(name):
        group = name[1]
        pieces = []
        for part in WINDOWS[name]:
            source, first = (halo, HALO[part]) if part in HALO else (segs, SEG[part])
            pieces.append(source[first : first + TALL[group], :])
        tokens = mul(gathers[group], jnp.concatenate(pieces, axis=0))
        wide = 128 if group != "B" else 256
        mask = head_cols[:, :128] if group != "B" else head_cols[:, 128:]
        for level in range(2):
            lo = SLOT[name] + level * wide
            level_tokens = jnp.concatenate([tokens[level * 72 : level * 72 + 72], tokens[144:]], axis=1)
            level_tokens = level_tokens.astype(BF16)
            keys = mul(level_tokens, w_keys[level]).astype(BF16)
            values_t = mul_t(w_values_t[level], level_tokens).astype(BF16)
            scores = mul_t(keys, queries[lo : lo + wide, :]) * SCALE + bias[:, lo : lo + wide]
            weights = jnp.exp(scores - jnp.max(scores, axis=0, keepdims=True))
            probs = weights * (1.0 / jnp.sum(weights, axis=0, keepdims=True))
            mixed[:, lo : lo + wide] = (mul(values_t, probs.astype(BF16)) * mask).astype(BF16)

    tables_in[1].wait()
    tab2[...] = jnp.zeros_like(tab2)
    for head in range(12):
        tab2[head : head + 1, :3312] = table_2[head]
    on_left = lon % 2 == 0
    rows2 = by_step(tab2[...], 23)
    copies[3].wait()
    pick2, rep_c, lane_c = const.pick2(), const.rep_c(), const.lane_c().astype(F32)
    for part in range(2):
        steps = rows2[96:272] if part == 0 else jnp.where(on_left, rows2[:176], rows2[192:])
        high, low = split(steps)
        value = merged((picked(pick2, high), picked(pick2, low)), rep_c, lane_c)
        for key_col in range(6):
            first = part * 72 + key_col * 12
            bias2[first : first + 12, :] = shifted(value, (5 - key_col) * 144, 896)[:12]

    sends[0].wait()
    sends[1].wait()
    attend("LB")
    attend("RB")
    table_copy.wait()
    value = merged((table_got[...],), rep_a, lane_a)
    lay_bias("A", jnp.where(jnp.logical_and(key_row < 3, lat == 0), -1e9, value))
    for send in sends[2:]:
        send.wait()
    for name in ("LC", "RC", "LA", "RA"):
        attend(name)

    heads = mul_t(const.collect(), mixed[...]).astype(BF16)
    hidden = own + mul(heads, get.w_proj1()[...])
    normed2 = norm(hidden, get.ln2_gain()[...]).astype(BF16)
    inner = mul(normed2, get.w_fc1()[...])
    expanded = (0.5 * inner * (1.0 + lax.erf(inner * (0.5**0.5)))).astype(BF16)
    fine = (hidden + mul_t(expanded, get.w_fc2()[...])).astype(BF16)
    fine_rows = mul(const.unperm(), fine)
    for token in range(144):
        fine_buf[token] = fine_rows[token * 2 : token * 2 + 2].astype(BF16)
    fine_out = pltpu.make_async_copy(fine_buf, fine_ref, out_sem.at[0])
    fine_out.start()

    fine = fine.astype(F32)
    patches = [fine[p * 72 : p * 72 + 72] for p in range(4)]
    total = sum(jnp.sum(p, axis=-1, keepdims=True) for p in patches)
    centred = [p - total * (1.0 / 768) for p in patches]
    total = sum(jnp.sum(p * p, axis=-1, keepdims=True) for p in centred)
    factor = lax.rsqrt(total * (1.0 / 768) + 1e-05)
    gain = get.merge_gain()[...]
    gain = jnp.concatenate([gain[i : i + 1] for i in range(6)], axis=1)
    gain = jnp.broadcast_to(gain, (8, 768))
    w_merge = get.w_merge()[...]
    coarse = None
    for p in range(4):
        part_gain = shifted(gain, p * 192, 192)[:1]
        part = (centred[p] * factor * part_gain).astype(BF16)
        term = mul(part, w_merge[p * 192 : p * 192 + 192])
        coarse = term if coarse is None else coarse + term
    coarse = coarse.astype(BF16)
    gain = get.ln3_gain()[...]
    gain = jnp.concatenate([gain[i : i + 1] for i in range(3)], axis=1)
    normed3 = norm(coarse.astype(F32), gain)
    rows_sent[...] = below(normed3, 80)
    partner = (lat, lon + 1 - 2 * lax.rem(lon, 2))
    swap = pltpu.make_async_remote_copy(
        src_ref=rows_sent, dst_ref=rows_got, send_sem=send_sem.at[9], recv_sem=recv_sem.at[9],
        device_id=partner, device_id_type=MESH,
    )
    swap.start()

    normed3 = normed3.astype(BF16)
    w_qkv2 = get.w_qkv2()
    w_key2 = w_qkv2[:, 384:768]
    w_value2_t = mul_t(unit(384), w_qkv2[:, 768:]).astype(BF16)
    own_queries2 = below(mul(normed3, w_qkv2[:, :384]), 128)
    queries2 = (mul(const.spread2(), own_queries2) * const.head_rows2().astype(F32)).astype(BF16)
    coarse_pad = mul(const.pad2(), below(coarse.astype(F32), 128))
    head_cols2, collect2, w_proj2 = const.head_cols2().astype(F32), const.collect2(), get.w_proj2()[...]

    def scored(tokens, part):
        keys = mul(tokens, w_key2).astype(BF16)
        return mul_t(keys, queries2) * SCALE + bias2[part * 72 : part * 72 + 72, :]

    scores_near = scored(normed3, 0)
    values_near = mul_t(w_value2_t, normed3).astype(BF16)
    swap.wait()
    other = rows_got[...].astype(F32)[:72].astype(BF16)
    scores_far = scored(other, 1)
    values_far = mul_t(w_value2_t, other).astype(BF16)
    top = jnp.maximum(
        jnp.max(scores_near, axis=0, keepdims=True), jnp.max(scores_far, axis=0, keepdims=True)
    )
    near = jnp.exp(scores_near - top)
    far = jnp.exp(scores_far - top)
    factor = 1.0 / (jnp.sum(near, axis=0, keepdims=True) + jnp.sum(far, axis=0, keepdims=True))
    blended = mul(values_near, (near * factor).astype(BF16)) + mul(values_far, (far * factor).astype(BF16))
    heads2 = mul_t(collect2, (blended * head_cols2).astype(BF16)).astype(BF16)
    result = coarse_pad + mul(heads2, w_proj2)
    for token in range(36):
        coarse_buf[token] = result[token * 2 : token * 2 + 2].astype(BF16)
    coarse_out = pltpu.make_async_copy(coarse_buf, coarse_ref, out_sem.at[1])
    coarse_out.start()
    fine_out.wait()
    coarse_out.wait()


def shards(
    fine_tokens, ln1_gain, w_qkv1, bias1, w_proj1, ln2_gain, w_fc1, w_fc2, merge_gain, w_merge,
    ln3_gain, w_qkv2, bias2, w_proj2,
):
    ops = dict(
        fine_tokens=fine_tokens.transpose(1, 2, 0, 3).reshape(144, 2, 192),
        ln1_gain=ln1_gain.reshape(1, 192), w_qkv1=w_qkv1, bias1=bias1.reshape(12, 1, 3312),
        w_proj1=w_proj1, ln2_gain=ln2_gain.reshape(1, 192), w_fc1=w_fc1, w_fc2=w_fc2.T,
        merge_gain=merge_gain.reshape(6, 128), w_merge=w_merge, ln3_gain=ln3_gain.reshape(3, 128),
        w_qkv2=w_qkv2, bias2=bias2.reshape(12, 1, 3312), w_proj2=w_proj2,
        pack=jnp.asarray(packed()[0]),
    )
    names = tuple(ops)
    any_space = pl.BlockSpec(memory_space=pl.ANY)
    scratch = [pltpu.VMEM(ops[name].shape, ops[name].dtype) for name in KEPT]
    scratch += [
        pltpu.VMEM(packed()[0].shape, BF16),
        pltpu.VMEM((8, 3328), F32),
        pltpu.VMEM((16, 3328), F32),
        pltpu.VMEM((288, 192), F32),
        pltpu.VMEM((SEG_ROWS, 128), BF16),
        pltpu.VMEM((HALO_ROWS, 128), BF16),
        pltpu.VMEM((48, 184), BF16),
        pltpu.VMEM((48, 184), BF16),
        pltpu.VMEM((12, 1, 3312), F32),
        pltpu.VMEM((12, 1, 3312), F32),
        pltpu.VMEM((LANES, 192), BF16),
        pltpu.VMEM((72, LANES), F32),
        pltpu.VMEM((144, 896), F32),
        pltpu.VMEM((192, LANES), BF16),
        pltpu.VMEM((80, 384), BF16),
        pltpu.VMEM((80, 384), BF16),
        pltpu.VMEM((144, 2, 192), BF16),
        pltpu.VMEM((36, 2, 384), BF16),
        pltpu.SemaphoreType.DMA((len(LOADED),)),
        pltpu.SemaphoreType.DMA((2,)),
        pltpu.SemaphoreType.DMA((2,)),
        pltpu.SemaphoreType.DMA((10,)),
        pltpu.SemaphoreType.DMA((10,)),
    ]
    fine, coarse = pl.pallas_call(
        functools.partial(kernel, names),
        out_shape=(
            pltpu.VMEM((144, 2, 192), BF16),
            pltpu.VMEM((36, 2, 384), BF16),
        ),
        in_specs=[pl.BlockSpec(memory_space=pl.ANY)] * len(names),
        out_specs=(any_space, any_space),
        scratch_shapes=scratch,
        compiler_params=pltpu.CompilerParams(
            collective_id=0, has_side_effects=True, vmem_limit_bytes=56 * 1024 * 1024
        ),
        cost_estimate=pl.CostEstimate(
            flops=2_000_000_000, bytes_accessed=12_000_000, transcendentals=1_000_000
        ),
    )(*ops.values())
    fine = fine.reshape(12, 12, 2, 192).transpose(2, 0, 1, 3)
    return fine, coarse.reshape(6, 6, 2, 384).transpose(2, 0, 1, 3)


def solution(mesh):
    whole, by_lat, grid = P(), P("lat", None, None, None), P(None, "lat", "lon", None)
    in_specs = (grid, whole, whole, by_lat) + (whole,) * 8 + (by_lat, whole)
    return jax.shard_map(
        shards, mesh=mesh, in_specs=in_specs, out_specs=(grid, grid), check_vma=False
    )
```

profile of v0, /device:TPU:1, one launch (start us, length us, event | category | flops | bytes accessed | tf_op | source)
XLA Modules:
  0.0 31.2 jit_solution(8744118744003551641)
XLA Ops:
  0.6 29.3 %shard_map.158 = (bf16[144,2,192]{2,1,0:T(2,128)(2,1)S(1)}, bf16[36,2,384]{2,1,0:T(2,128)(2,1)S(1)}) custom-call(bf16[144,2,192]{2,1,0:T(2,128)(2,1)} %bitcast.21, f32[1,192]{1,0:T(1,128)} %bitcast.24, bf16[192,576]{1,0:T(8,128)(2,1)} %refs_2_.1, f32[12,1,3312]{2,1,0:T(1,128)} %bitcast.19, bf16[192,192]{1,0:T(8,128)(2,1)} %refs_4_.1, f32[1,192]{1,0:T(1,128)} %bitcast.25, ...), custom_call_target="tpu_custom_call" | custom-call | flops 2000000000 | bytes 12000000 | tf_op jit(solution)/shard_map/pallas_call | solution.py:571
  29.9 0.7 %copy.19 = bf16[2,12,12,192]{3,0,2,1:T(2,128)(2,1)} copy(bf16[2,12,12,192]{3,0,2,1:T(2,128)(2,1)S(1)} %bitcast.16) | data formatting | bytes 221184
  30.6 0.6 %copy.20 = bf16[2,6,6,384]{3,0,2,1:T(2,128)(2,1)} copy(bf16[2,6,6,384]{3,0,2,1:T(2,128)(2,1)S(1)} %bitcast.17) | data formatting | bytes 110592
where the time goes:
time: 31.3 us; the launch traced here: 31.2 us
  Pallas kernels  29.3 us (94%)
  local copies, waits for them, and re-layouts  1.29 us (4%)
  between operations  0.64 us (2%)
    pallas_call x1, Pallas kernels, shards(): pl.pallas_call(functools.partial(kernel, names), out_shape=(pltpu.VMEM((1...  29.3 us
    unnamed x2, local copies, waits for them, and re-layouts  1.29 us

commit v1 on v0

--- a/solution.py
+++ b/solution.py
@@ -252,7 +252,7 @@
     rest = list(refs[count + 2 :])
     loaded = SimpleNamespace(**dict(zip(KEPT, rest[: len(KEPT)])))
     (pack, tab, tab2, own_rows, segs, halo, table_sent, table_got, table_in, table_2, queries, bias,
-     bias2, mixed, rows_sent, rows_got, fine_buf, coarse_buf, load_sem, tab_sem, out_sem, send_sem,
+     bias2, mixed, rows_sent, rows_got, load_sem, tab_sem, send_sem,
      recv_sem) = rest[len(KEPT) :]
     _, place, ranges = packed()
 
@@ -440,10 +440,27 @@
             first = part * 72 + key_col * 12
             bias2[first : first + 12, :] = shifted(value, (5 - key_col) * 144, 896)[:12]
 
+    w_proj1, w_fc1, w_fc2 = get.w_proj1(), get.w_fc1(), get.w_fc2()
+    gain2 = get.ln2_gain()[...]
+    merge_gain = get.merge_gain()[...]
+    merge_gain = jnp.concatenate([merge_gain[i : i + 1] for i in range(6)], axis=1)
+    merge_gain = jnp.broadcast_to(merge_gain, (8, 768))
+    w_merge = get.w_merge()
+    gain3 = get.ln3_gain()[...]
+    gain3 = jnp.concatenate([gain3[i : i + 1] for i in range(3)], axis=1)
+    w_qkv2, w_proj2 = get.w_qkv2(), get.w_proj2()
+    w_value2_t = mul_t(unit(384), w_qkv2[:, 768:]).astype(BF16)
+
     sends[0].wait()
     sends[1].wait()
     attend("LB")
     attend("RB")
+    collect = const.collect()
+
+    def collected(first, end):
+        return mul_t(collect[:, first:end], mixed[:, first:end])
+
+    heads = collected(SLOT["LB"], SLOT["LC"]) + collected(SLOT["RB"], SLOT["RC"])
     table_copy.wait()
     value = merged((table_got[...],), rep_a, lane_a)
     lay_bias("A", jnp.where(jnp.logical_and(key_row < 3, lat == 0), -1e9, value))
@@ -452,38 +469,27 @@
     for name in ("LC", "RC", "LA", "RA"):
         attend(name)
 
-    heads = mul_t(const.collect(), mixed[...]).astype(BF16)
-    hidden = own + mul(heads, get.w_proj1()[...])
-    normed2 = norm(hidden, get.ln2_gain()[...]).astype(BF16)
-    inner = mul(normed2, get.w_fc1()[...])
+    heads += collected(0, SLOT["LB"]) + collected(SLOT["LC"], SLOT["RB"]) + collected(SLOT["RC"], LANES)
+    hidden = own + mul(heads.astype(BF16), w_proj1[...])
+    normed2 = norm(hidden, gain2).astype(BF16)
+    inner = mul(normed2, w_fc1[...])
     expanded = (0.5 * inner * (1.0 + lax.erf(inner * (0.5**0.5)))).astype(BF16)
-    fine = (hidden + mul_t(expanded, get.w_fc2()[...])).astype(BF16)
-    fine_rows = mul(const.unperm(), fine)
-    for token in range(144):
-        fine_buf[token] = fine_rows[token * 2 : token * 2 + 2].astype(BF16)
-    fine_out = pltpu.make_async_copy(fine_buf, fine_ref, out_sem.at[0])
-    fine_out.start()
-
-    fine = fine.astype(F32)
+    fine_rows = (hidden + mul_t(expanded, w_fc2[...])).astype(BF16)
+
+    fine = fine_rows.astype(F32)
     patches = [fine[p * 72 : p * 72 + 72] for p in range(4)]
     total = sum(jnp.sum(p, axis=-1, keepdims=True) for p in patches)
     centred = [p - total * (1.0 / 768) for p in patches]
     total = sum(jnp.sum(p * p, axis=-1, keepdims=True) for p in centred)
     factor = lax.rsqrt(total * (1.0 / 768) + 1e-05)
-    gain = get.merge_gain()[...]
-    gain = jnp.concatenate([gain[i : i + 1] for i in range(6)], axis=1)
-    gain = jnp.broadcast_to(gain, (8, 768))
-    w_merge = get.w_merge()[...]
     coarse = None
     for p in range(4):
-        part_gain = shifted(gain, p * 192, 192)[:1]
+        part_gain = shifted(merge_gain, p * 192, 192)[:1]
         part = (centred[p] * factor * part_gain).astype(BF16)
         term = mul(part, w_merge[p * 192 : p * 192 + 192])
         coarse = term if coarse is None else coarse + term
     coarse = coarse.astype(BF16)
-    gain = get.ln3_gain()[...]
-    gain = jnp.concatenate([gain[i : i + 1] for i in range(3)], axis=1)
-    normed3 = norm(coarse.astype(F32), gain)
+    normed3 = norm(coarse.astype(F32), gain3)
     rows_sent[...] = below(normed3, 80)
     partner = (lat, lon + 1 - 2 * lax.rem(lon, 2))
     swap = pltpu.make_async_remote_copy(
@@ -493,20 +499,20 @@
     swap.start()
 
     normed3 = normed3.astype(BF16)
-    w_qkv2 = get.w_qkv2()
-    w_key2 = w_qkv2[:, 384:768]
-    w_value2_t = mul_t(unit(384), w_qkv2[:, 768:]).astype(BF16)
     own_queries2 = below(mul(normed3, w_qkv2[:, :384]), 128)
     queries2 = (mul(const.spread2(), own_queries2) * const.head_rows2().astype(F32)).astype(BF16)
     coarse_pad = mul(const.pad2(), below(coarse.astype(F32), 128))
-    head_cols2, collect2, w_proj2 = const.head_cols2().astype(F32), const.collect2(), get.w_proj2()[...]
+    head_cols2, collect2 = const.head_cols2().astype(F32), const.collect2()
 
     def scored(tokens, part):
-        keys = mul(tokens, w_key2).astype(BF16)
+        keys = mul(tokens, w_qkv2[:, 384:768]).astype(BF16)
         return mul_t(keys, queries2) * SCALE + bias2[part * 72 : part * 72 + 72, :]
 
     scores_near = scored(normed3, 0)
     values_near = mul_t(w_value2_t, normed3).astype(BF16)
+    placed_rows = mul(const.unperm(), fine_rows)
+    for token in range(144):
+        fine_ref[token] = placed_rows[token * 2 : token * 2 + 2].astype(BF16)
     swap.wait()
     other = rows_got[...].astype(F32)[:72].astype(BF16)
     scores_far = scored(other, 1)
@@ -519,13 +525,9 @@
     factor = 1.0 / (jnp.sum(near, axis=0, keepdims=True) + jnp.sum(far, axis=0, keepdims=True))
     blended = mul(values_near, (near * factor).astype(BF16)) + mul(values_far, (far * factor).astype(BF16))
     heads2 = mul_t(collect2, (blended * head_cols2).astype(BF16)).astype(BF16)
-    result = coarse_pad + mul(heads2, w_proj2)
+    result = coarse_pad + mul(heads2, w_proj2[...])
     for token in range(36):
-        coarse_buf[token] = result[token * 2 : token * 2 + 2].astype(BF16)
-    coarse_out = pltpu.make_async_copy(coarse_buf, coarse_ref, out_sem.at[1])
-    coarse_out.start()
-    fine_out.wait()
-    coarse_out.wait()
+        coarse_ref[token] = result[token * 2 : token * 2 + 2].astype(BF16)
 
 
 def shards(
@@ -560,10 +562,7 @@
         pltpu.VMEM((192, LANES), BF16),
         pltpu.VMEM((80, 384), BF16),
         pltpu.VMEM((80, 384), BF16),
-        pltpu.VMEM((144, 2, 192), BF16),
-        pltpu.VMEM((36, 2, 384), BF16),
         pltpu.SemaphoreType.DMA((len(LOADED),)),
-        pltpu.SemaphoreType.DMA((2,)),
         pltpu.SemaphoreType.DMA((2,)),
         pltpu.SemaphoreType.DMA((10,)),
         pltpu.SemaphoreType.DMA((10,)),
@@ -575,7 +574,7 @@
             pltpu.VMEM((36, 2, 384), BF16),
         ),
         in_specs=[pl.BlockSpec(memory_space=pl.ANY)] * len(names),
-        out_specs=(any_space, any_space),
+        out_specs=(pl.BlockSpec(memory_space=pltpu.VMEM),) * 2,
         scratch_shapes=scratch,
         compiler_params=pltpu.CompilerParams(
             collective_id=0, has_side_effects=True, vmem_limit_bytes=56 * 1024 * 1024

time: 31.3 us -> 30.8 us (0.984)
  Pallas kernels: 29.3 us -> 28.8 us
    pallas_call x1, Pallas kernels: 29.3 us -> 28.8 us  [shards(): pl.pallas_call(functools.partial(kernel, names), out_shape=(pltpu.VMEM((1...]
where the time goes in v1:
time: 30.8 us; the launch traced here: 30.7 us
  Pallas kernels  28.8 us (94%)
  local copies, waits for them, and re-layouts  1.29 us (4%)
  between operations  0.64 us (2%)
    pallas_call x1, Pallas kernels, shards(): pl.pallas_call(functools.partial(kernel, names), out_shape=(pltpu.VMEM((1...  28.8 us
    unnamed x2, local copies, waits for them, and re-layouts  1.29 us

profile of v1, /device:TPU:1, one launch (start us, length us, event | category | flops | bytes accessed | tf_op | source)
XLA Modules:
  0.0 30.7 jit_solution(12575545908935119387)
XLA Ops:
  0.6 28.8 %shard_map.158 = (bf16[144,2,192]{2,1,0:T(2,128)(2,1)S(1)}, bf16[36,2,384]{2,1,0:T(2,128)(2,1)S(1)}) custom-call(bf16[144,2,192]{2,1,0:T(2,128)(2,1)} %bitcast.21, f32[1,192]{1,0:T(1,128)} %bitcast.24, bf16[192,576]{1,0:T(8,128)(2,1)} %refs_2_.1, f32[12,1,3312]{2,1,0:T(1,128)} %bitcast.19, bf16[192,192]{1,0:T(8,128)(2,1)} %refs_4_.1, f32[1,192]{1,0:T(1,128)} %bitcast.25, ...), custom_call_target="tpu_custom_call" | custom-call | flops 2000000000 | bytes 12000000 | tf_op jit(solution)/shard_map/pallas_call | solution.py:570
  29.4 0.7 %copy.19 = bf16[2,12,12,192]{3,0,2,1:T(2,128)(2,1)} copy(bf16[2,12,12,192]{3,0,2,1:T(2,128)(2,1)S(1)} %bitcast.16) | data formatting | bytes 221184
  30.1 0.6 %copy.20 = bf16[2,6,6,384]{3,0,2,1:T(2,128)(2,1)} copy(bf16[2,6,6,384]{3,0,2,1:T(2,128)(2,1)S(1)} %bitcast.17) | data formatting | bytes 110592
